TPU v7x, 256 devices: a whole 4x4x8 slice. The times are simulated.
256 devices in a mesh: tm: 32 (over z, y), clip: 8 (over x, core).
Axes of the slice: x: 4, y: 4, z: 8, core: 2. Of those that a mesh axis runs over, the one named last changes fastest.
Arguments:
- block_input: bfloat16 [8, 128, 16, 16, 256], P('clip', 'tm'), may hold values from -6 to 6
- pre_act: bfloat16 [8, 128, 16, 16, 512], P('clip', 'tm'), may hold values from -6 to 6
- time_out: bfloat16 [8, 128, 16, 16, 512], P('clip', 'tm'), may hold values from -6 to 6
- w_space: bfloat16 [256, 3, 3, 512], replicated, may hold values from -0.125 to 0.125
- w_time: bfloat16 [512, 3, 512], replicated, may hold values from -0.15625 to 0.15625
- proj: bfloat16 [512, 18], replicated, may hold values from -0.25 to 0.25
- codes: int32 [8, 128, 16, 16], P('clip', 'tm'), may hold values from 0 to 262143
- cotan: bfloat16 [8, 128, 16, 16, 18], P('clip', 'tm'), may hold values from -6 to 6
- lengths: int32 [8], replicated, may hold values from 1 to 128
Outputs:
- grad_input: bfloat16 [8, 128, 256, 256], P('clip', None, 'tm')
- grad_space: float32 [256, 3, 3, 512], P('tm')
- grad_time: float32 [512, 3, 512], P('tm')
- grad_proj: float32 [512, 18], P('tm')
All inputs are finite; a program needn't handle non-finite values.
Results may differ from a plain program's by a relative error of at most 0.025.
Values may be sent and summed in bfloat16 or wider, within the bound.
A program may use at most 64 MiB of HBM per device.

v0:
```python
import math
import jax
import jax.numpy as jnp
from jax import lax
from jax.sharding import PartitionSpec as P

commit_weight = 0.25


def from_behind(shard, axis, by):
    devices = lax.axis_size(axis)
    pairs = [(i, i + by) for i in range(devices) if 0 <= i + by < devices]
    return lax.ppermute(shard, axis, pairs)


def shift_space(values, down, right):
    side_len = values.shape[-2]
    padded = jnp.pad(values, ((0, 0), (1, 1), (1, 1), (0, 0)))
    return padded[:, 1 + down : 1 + down + side_len, 1 + right : 1 + right + side_len, :]


def silu_slope(pre):
    sigma = jax.nn.sigmoid(pre)
    return sigma * (1.0 + pre * (1.0 - sigma))


def sign_targets(flat_codes, latent):
    powers = (2 ** jnp.arange(latent)).astype(jnp.int32)
    bits = flat_codes[:, None] // powers[None, :] % 2
    return 2.0 * bits.astype(jnp.float32) - 1.0


def per_device(block_input, pre_act, time_out, w_space, w_time, proj, codes, cotan, lengths):
    clip_x = block_input[0]
    clip_pre = pre_act[0]
    frames_dev, side_len, _, cin = clip_x.shape
    cmid = clip_pre.shape[-1]
    latent = proj.shape[1]
    positions = side_len * side_len
    rows = frames_dev * positions
    slab_count = lax.axis_size("tm")
    group_count = lax.axis_size("clip")
    scale = 1.0 / math.sqrt(group_count * slab_count * rows)
    clip_len = lax.dynamic_index_in_dim(lengths, lax.axis_index("clip"), 0, keepdims=False)
    frame_ids = lax.axis_index("tm") * frames_dev + jnp.arange(frames_dev)
    live = (frame_ids < clip_len).astype(jnp.float32)
    live_rows = jnp.repeat(live, positions)[:, None]
    t_rows = time_out[0].reshape(rows, cmid)
    latent_z = jnp.dot(t_rows, proj, preferred_element_type=jnp.float32)
    targets = sign_targets(codes[0].reshape(rows), latent)
    grad_z = (
        live_rows
        * (
            cotan[0].reshape(rows, latent).astype(jnp.float32)
            + 2.0 * commit_weight * (latent_z - targets)
        )
    ).astype(jnp.bfloat16)
    proj_part = jnp.dot(t_rows.T, grad_z, preferred_element_type=jnp.float32)
    grad_t = jnp.dot(grad_z, proj.T, preferred_element_type=jnp.float32).astype(jnp.bfloat16)
    grad_t = grad_t.reshape(frames_dev, positions, cmid)
    grad_t_rows = grad_t.reshape(rows, cmid)
    next_frames = from_behind(grad_t[:2], "tm", -1)
    t_ext = jnp.concatenate([grad_t, next_frames], axis=0)
    act = (
        jax.nn.silu(clip_pre.astype(jnp.float32))
        .astype(jnp.bfloat16)
        .reshape(frames_dev, positions, cmid)
    )
    grad_act = jnp.zeros((rows, cmid), jnp.float32)
    for lag in range(3):
        ahead = t_ext[lag : lag + frames_dev].reshape(rows, cmid)
        grad_act = grad_act + jnp.dot(
            ahead, w_time[:, lag, :].T, preferred_element_type=jnp.float32
        )
    time_terms = []
    prev_frames = from_behind(act[frames_dev - 2 :], "tm", 1)
    a_ext = jnp.concatenate([prev_frames, act], axis=0)
    for lag in range(3):
        behind = a_ext[2 - lag : 2 - lag + frames_dev].reshape(rows, cmid)
        time_terms.append(jnp.dot(behind.T, grad_t_rows, preferred_element_type=jnp.float32))
    time_part = jnp.stack(time_terms, axis=1)
    grad_pre = (
        grad_act.reshape(frames_dev, side_len, side_len, cmid)
        * silu_slope(clip_pre.astype(jnp.float32))
    ).astype(jnp.bfloat16)
    pre_rows = grad_pre.reshape(rows, cmid)
    grad_x = jnp.zeros((frames_dev, side_len, side_len, cin), jnp.float32)
    space_rows = []
    for row_tap in range(3):
        row_terms = []
        for col_tap in range(3):
            moved = shift_space(clip_x, row_tap - 1, col_tap - 1).reshape(rows, cin)
            row_terms.append(jnp.dot(moved.T, pre_rows, preferred_element_type=jnp.float32))
            back = jnp.dot(
                pre_rows, w_space[:, row_tap, col_tap, :].T, preferred_element_type=jnp.float32
            )
            grad_x = grad_x + shift_space(
                back.reshape(frames_dev, side_len, side_len, cin), 1 - row_tap, 1 - col_tap
            )
        space_rows.append(jnp.stack(row_terms, axis=1))
    space_part = jnp.stack(space_rows, axis=1)
    grad_cells = grad_x.astype(jnp.bfloat16).reshape(1, frames_dev, positions, cin)
    grad_input = lax.all_to_all(grad_cells, "tm", split_axis=2, concat_axis=1, tiled=True)
    space_part = space_part * scale
    time_part = time_part * scale
    proj_part = proj_part * scale
    summed = (
        lax.psum(space_part.astype(jnp.bfloat16), "clip").astype(jnp.float32),
        lax.psum(time_part.astype(jnp.bfloat16), "clip").astype(jnp.float32),
        lax.psum(proj_part.astype(jnp.bfloat16), "clip").astype(jnp.float32),
    )
    owned = (
        lax.psum_scatter(
            summed[0].astype(jnp.bfloat16), "tm", scatter_dimension=0, tiled=True
        ).astype(jnp.float32),
        lax.psum_scatter(
            summed[1].astype(jnp.bfloat16), "tm", scatter_dimension=0, tiled=True
        ).astype(jnp.float32),
        lax.psum_scatter(
            summed[2].astype(jnp.bfloat16), "tm", scatter_dimension=0, tiled=True
        ).astype(jnp.float32),
    )
    return (grad_input, owned[0], owned[1], owned[2])


def solution(mesh):
    placed = (
        P("clip", "tm", None, None, None),
        P("clip", "tm", None, None, None),
        P("clip", "tm", None, None, None),
        P(),
        P(),
        P(),
        P("clip", "tm", None, None),
        P("clip", "tm", None, None, None),
        P(),
    )
    return jax.shard_map(
        per_device,
        mesh=mesh,
        in_specs=placed,
        out_specs=(
            P("clip", None, "tm", None),
            P("tm", None, None, None),
            P("tm", None, None),
            P("tm", None),
        ),
        check_vma=False,
    )
```

profile of v0, /device:TPU:1, one launch (start us, length us, event | category | flops | bytes accessed | tf_op | source)
XLA Modules:
  0.0 757.8 jit_solution(11394494174237194665)
XLA Ops:
  7.3 1.3 dynamic_slice.4
  10.1 1.0 bitcast_convert_fusion
  11.3 2.0 fusion.18
  13.9 1.3 collective-permute-start
  15.9 11.3 %collective-permute-done = bf16[2,256,512]{2,1,0:T(8,128)(2,1)S(1)} collective-permute-done((bf16[2,256,512]{2,1,0:T(8,128)(2,1)S(1)}, bf16[2,256,512]{2,1,0:T(8,128)(2,1)S(1)}, u32[]{:S(2)}, u32[]{:S(2)}) %collective-permute-start) | collective-permute-done | bytes 524320 | tf_op jit(solution)/shard_map/ppermute | solution.py:13
  28.7 2.5 fusion.9
  31.2 2.2 add_divide_fusion
  38.7 3.7 copy.45
  42.4 7.4 reshape.147
  51.1 1.7 convert_bitcast_fusion
  53.7 5.4 collective-permute-start.1
  59.8 2.4 fusion.35
  62.3 6.5 collective-permute-done.1
  70.4 1.6 fusion.1
  72.0 1.6 fusion.37
  77.7 1.2 copy.22
  78.9 14.4 %all-to-all-start = ((bf16[1,4,256,256]{3,1,0,2:T(4,128)(2,1)}), bf16[1,4,256,256]{3,1,0,2:T(4,128)(2,1)S(1)}, u32[]{:S(2)}, u32[]{:S(2)}) async-start(bf16[1,4,256,256]{3,1,0,2:T(4,128)(2,1)} %copy.22), calls=%async_computation | async-start | bytes 1048576 | tf_op jit(solution)/shard_map/all_to_all | solution.py:103
  93.4 177.9 %reduce-scatter.10.cloned.1.call-done = bf16[8,4608]{1,0:T(8,128)(2,1)} async-done(((bf16[256,4608]{1,0:T(8,128)(2,1)}), bf16[8,4608]{1,0:T(8,128)(2,1)}) %reduce-scatter.10.cloned.1.call-update) | async-done | bytes 73744
  271.4 194.6 %reduce-scatter.12.cloned.1.call-done = bf16[16,18]{1,0:T(8,128)(2,1)} async-done(((bf16[512,18]{1,0:T(8,128)(2,1)}), bf16[16,18]{1,0:T(8,128)(2,1)}) %reduce-scatter.12.cloned.1.call-update) | async-done | bytes 592
  466.7 0.9 copy.23
  467.6 216.4 %reduce-scatter.8.cloned.1.call-done = bf16[16,3,512]{2,0,1:T(8,128)(2,1)} async-done(((bf16[512,3,512]{2,0,1:T(8,128)(2,1)}), bf16[16,3,512]{2,0,1:T(8,128)(2,1)}) %reduce-scatter.8.cloned.1.call-update) | async-done | bytes 49168 | tf_op jit(solution)/shard_map/reduce_scatter | solution.py:116
  684.0 27.6 %all-reduce.9 = (bf16[16,18]{0,1:T(8,128)(2,1)S(1)}, bf16[16,3,512]{2,0,1:T(8,128)(2,1)S(1)}) all-reduce(bf16[16,18]{0,1:T(8,128)(2,1)S(1)} %copy.48, bf16[16,3,512]{2,0,1:T(8,128)(2,1)} %reduce-scatter.8.cloned.1.call-done), channel_id=1, replica_groups=mesh['tm'=32,'clip'=8] {'clip'}, use_global_device_ids=true, to_apply=%region_4.5 | all-reduce | flops 24864 | bytes 99456 | tf_op jit(solution)/shard_map/psum | solution.py:110
  712.9 36.9 %all-reduce.12.cloned.1.call-done = bf16[8,3,3,512]{3,0,2,1:T(8,128)(2,1)} async-done(((bf16[8,3,3,512]{3,0,2,1:T(8,128)(2,1)}), bf16[8,3,3,512]{3,0,2,1:T(8,128)(2,1)}) %all-reduce.12.cloned.1.call-update) | async-done | bytes 73744 | tf_op jit(solution)/shard_map/psum | solution.py:108
  749.7 1.6 convert_element_type.117
  (72 shorter events, 20.5 us)
Async XLA Ops:
  7.2 4.2 copy-start
  7.2 6.2 copy-start.8
  7.2 264.1 %reduce-scatter.10.cloned.1.call-start = ((), (), s32[]{:S(2)}) async-start(), calls=%async_computation.6 | async-start | bytes 2433024
  11.3 3.9 copy-start.6
  13.9 13.4 %collective-permute-start = (bf16[2,256,512]{2,1,0:T(8,128)(2,1)S(1)}, bf16[2,256,512]{2,1,0:T(8,128)(2,1)S(1)}, u32[]{:S(2)}, u32[]{:S(2)}) collective-permute-start(bf16[2,256,512]{2,1,0:T(8,128)(2,1)S(1)} %bitcast.259), channel_id=1, source_target_pairs={{8,0},{16,8},{24,16},{32,24},{40,32},{48,40},{56,48},{64,56},{72,6... | collective-permute-start | bytes 1572872 | tf_op jit(solution)/shard_map/ppermute | solution.py:13
  27.5 1.2 copy-start.1
  31.2 2.2 copy-start.7
  49.8 416.2 %reduce-scatter.12.cloned.1.call-start = ((), (), s32[]{:S(2)}) async-start(), calls=%async_computation.7 | async-start | bytes 135168
  50.9 633.1 %reduce-scatter.8.cloned.1.call-start = ((), (), s32[]{:S(2)}) async-start(), calls=%async_computation.5 | async-start | bytes 1622016 | tf_op jit(solution)/shard_map/reduce_scatter | solution.py:116
  51.1 1.7 copy-start.2
  51.1 2.3 copy-start.3
  52.8 6.3 copy-start.9
  53.7 15.0 %collective-permute-start.1 = (bf16[2,256,512]{2,1,0:T(8,128)(2,1)S(1)}, bf16[2,256,512]{2,1,0:T(8,128)(2,1)S(1)}, u32[]{:S(2)}, u32[]{:S(2)}) collective-permute-start(bf16[2,256,512]{2,1,0:T(8,128)(2,1)S(1)} %bitcast.257), channel_id=1, source_target_pairs={{0,8},{8,16},{16,24},{24,32},{32,40},{40,48},{48,56},{56,64},{64,7... | collective-permute-start | bytes 1572872 | tf_op jit(solution)/shard_map/ppermute | solution.py:13
  72.0 1.7 copy-start.5
  75.7 1.2 copy-start.4
  78.9 387.8 %all-to-all-start = ((bf16[1,4,256,256]{3,1,0,2:T(4,128)(2,1)}), bf16[1,4,256,256]{3,1,0,2:T(4,128)(2,1)S(1)}, u32[]{:S(2)}, u32[]{:S(2)}) async-start(bf16[1,4,256,256]{3,1,0,2:T(4,128)(2,1)} %copy.22), calls=%async_computation | async-start | bytes 1048576 | tf_op jit(solution)/shard_map/all_to_all | solution.py:103
  93.4 656.3 %all-reduce.12.cloned.1.call-start = ((), (), s32[]{:S(2)}) async-start(), calls=%async_computation.4 | async-start | bytes 147456 | tf_op jit(solution)/shard_map/psum | solution.py:108
Sparse Core Ops, SparseCore 0:
  49.9 221.4 reduce-scatter.9
  275.5 190.3 reduce-scatter.11
  470.2 213.6 reduce-scatter.7
  686.3 63.3 all-reduce.11
where the time goes:
time: 759 us; the launch traced here: 758 us
  waiting for transfers between devices  644 us (85%)
  blocking collectives  27.6 us (4%)
  starting transfers between devices  21.4 us (3%)
  matrix products  20.7 us (3%)
  local copies, waits for them, and re-layouts  18.8 us (2%)
  between operations  14.2 us (2%)
  other arithmetic  11.6 us (2%)
    unnamed x6, waiting for transfers between devices  373 us
    reduce_scatter x1, waiting for transfers between devices, per_device(): lax.psum_scatter(summed[1].astype(jnp.bfloat16), 'tm', scatter_dimension=...  216 us
    psum x1, waiting for transfers between devices, per_device(): lax.psum(space_part.astype(jnp.bfloat16), 'clip').astype(jnp.float32)  36.9 us
    psum x1, blocking collectives, per_device(): lax.psum(proj_part.astype(jnp.bfloat16), 'clip').astype(jnp.float32)  27.6 us
    ppermute x2, waiting for transfers between devices, from_behind(): return lax.ppermute(shard, axis, pairs)  17.8 us
  transfers between devices with their start and end apart: 7, of which 6 were waited for; matrix products, arithmetic and copies ran while one was open for 3% of the time, Pallas kernels for 0%

commit v1 on v0

--- a/solution.py
+++ b/solution.py
@@ -104,8 +104,11 @@
     space_part = space_part * scale
     time_part = time_part * scale
     proj_part = proj_part * scale
+    number_gates_up = lambda inputs, link_axis: jnp.sum(
+        lax.all_gather(inputs, axis_name=link_axis), 0
+    )
     summed = (
-        lax.psum(space_part.astype(jnp.bfloat16), "clip").astype(jnp.float32),
+        number_gates_up(space_part.astype(jnp.bfloat16), link_axis="clip").astype(jnp.float32),
         lax.psum(time_part.astype(jnp.bfloat16), "clip").astype(jnp.float32),
         lax.psum(proj_part.astype(jnp.bfloat16), "clip").astype(jnp.float32),
     )

time: 759 us -> 693 us (0.913)
  waiting for transfers between devices: 644 us -> 564 us
  other arithmetic: 11.6 us -> 24.9 us
    unnamed x6, waiting for transfers between devices: 373 us -> 245 us
    all_gather x0 -> x1, waiting for transfers between devices: none -> 82.9 us  [per_device(): lax.all_gather(inputs, axis_name=link_axis)]
    psum x1 -> x0, waiting for transfers between devices: 36.9 us -> none  [per_device(): lax.psum(space_part.astype(jnp.bfloat16), 'clip').astype(jnp.float32)]
    reduce_sum x0 -> x1, other arithmetic: none -> 11.9 us  [per_device(): jnp.sum(lax.all_gather(inputs, axis_name=link_axis), 0)]
    unnamed x27 -> x25, local copies, waits for them, and re-layouts: 14.3 us -> 15.9 us
  transfers between devices with their start and end apart: 7 -> 7, of which waited for: 6 -> 6; matrix products, arithmetic and copies ran while one was open for 3% -> 6% of each run, Pallas kernels for 0% -> 0%
where the time goes in v1:
time: 693 us; the launch traced here: 688 us
  waiting for transfers between devices  564 us (81%)
  blocking collectives  27.5 us (4%)
  other arithmetic  24.9 us (4%)
  local copies, waits for them, and re-layouts  20.4 us (3%)
  matrix products  18.6 us (3%)
  starting transfers between devices  16.7 us (2%)
  between operations  16 us (2%)
    unnamed x6, waiting for transfers between devices  245 us
    reduce_scatter x1, waiting for transfers between devices, per_device(): lax.psum_scatter(summed[1].astype(jnp.bfloat16), 'tm', scatter_dimension=...  217 us
    all_gather x1, waiting for transfers between devices, per_device(): lax.all_gather(inputs, axis_name=link_axis)  82.9 us
    psum x1, blocking collectives, per_device(): lax.psum(proj_part.astype(jnp.bfloat16), 'clip').astype(jnp.float32)  27.5 us
    ppermute x2, waiting for transfers between devices, from_behind(): return lax.ppermute(shard, axis, pairs)  19.4 us
    unnamed x25, local copies, waits for them, and re-layouts  15.9 us
  transfers between devices with their start and end apart: 7, of which 6 were waited for; matrix products, arithmetic and copies ran while one was open for 6% of the time, Pallas kernels for 0%

profile of v1, /device:TPU:1, one launch (start us, length us, event | category | flops | bytes accessed | tf_op | source)
XLA Modules:
  0.0 688.0 jit_solution(15908798638807486840)
XLA Ops:
  8.1 1.3 dynamic_slice.4
  11.0 1.0 bitcast_convert_fusion
  12.2 2.0 fusion.18
  14.7 1.3 collective-permute-start
  16.8 11.4 %collective-permute-done = bf16[2,256,512]{2,1,0:T(8,128)(2,1)S(1)} collective-permute-done((bf16[2,256,512]{2,1,0:T(8,128)(2,1)S(1)}, bf16[2,256,512]{2,1,0:T(8,128)(2,1)S(1)}, u32[]{:S(2)}, u32[]{:S(2)}) %collective-permute-start) | collective-permute-done | bytes 524320 | tf_op jit(solution)/shard_map/ppermute | solution.py:13
  29.5 2.3 fusion.9
  31.9 2.3 add_divide_fusion
  38.8 2.1 fusion
  42.1 1.7 convert_bitcast_fusion
  44.2 5.7 collective-permute-start.1
  51.3 8.1 %collective-permute-done.1 = bf16[2,256,512]{2,1,0:T(8,128)(2,1)S(1)} collective-permute-done((bf16[2,256,512]{2,1,0:T(8,128)(2,1)S(1)}, bf16[2,256,512]{2,1,0:T(8,128)(2,1)S(1)}, u32[]{:S(2)}, u32[]{:S(2)}) %collective-permute-start.1) | collective-permute-done | bytes 524320 | tf_op jit(solution)/shard_map/ppermute | solution.py:13
  61.0 1.6 fusion.1
  62.7 82.9 %all-gather.2.cloned.1.call-done = bf16[8,256,3,3,512]{4,1,3,2,0:T(8,128)(2,1)} async-done(((bf16[1,256,3,3,512]{4,1,3,2,0:T(8,128)(2,1)}), bf16[8,256,3,3,512]{4,1,3,2,0:T(8,128)(2,1)}) %all-gather.2.cloned.1.call-update) | async-done | bytes 18874384 | tf_op jit(solution)/shard_map/all_gather | solution.py:108
  145.6 11.9 %reduce_sum.12 = bf16[256,3,3,512]{3,0,2,1:T(8,128)(2,1)} reduce(bf16[8,256,3,3,512]{4,1,3,2,0:T(8,128)(2,1)} %all-gather.2.cloned.1.call-done, bf16[]{:T(256)} %constant.76.clone.1), dimensions={0}, to_apply=%region_0.1 | reduce | flops 8257536 | bytes 21233666 | tf_op jit(solution)/shard_map/reduce_sum | solution.py:107
  157.6 5.3 copy.45
  162.9 7.4 %reshape.195 = bf16[256,4608]{1,0:T(8,128)(2,1)} reshape(bf16[256,3,3,512]{3,2,1,0:T(4,128)(2,1)} %copy.45) | data formatting | bytes 4718592
  170.3 1.6 fusion.35
  176.2 1.2 copy.22
  177.4 9.6 %all-to-all-start = ((bf16[1,4,256,256]{3,1,0,2:T(4,128)(2,1)}), bf16[1,4,256,256]{3,1,0,2:T(4,128)(2,1)S(1)}, u32[]{:S(2)}, u32[]{:S(2)}) async-start(bf16[1,4,256,256]{3,1,0,2:T(4,128)(2,1)} %copy.22), calls=%async_computation | async-start | bytes 1048576 | tf_op jit(solution)/shard_map/all_to_all | solution.py:103
  186.9 54.0 %reduce-scatter.12.cloned.1.call-done = bf16[16,18]{1,0:T(8,128)(2,1)} async-done(((bf16[512,18]{1,0:T(8,128)(2,1)}), bf16[16,18]{1,0:T(8,128)(2,1)}) %reduce-scatter.12.cloned.1.call-update) | async-done | bytes 592
  242.6 216.5 %reduce-scatter.8.cloned.1.call-done = bf16[16,3,512]{2,0,1:T(8,128)(2,1)} async-done(((bf16[512,3,512]{2,0,1:T(8,128)(2,1)}), bf16[16,3,512]{2,0,1:T(8,128)(2,1)}) %reduce-scatter.8.cloned.1.call-update) | async-done | bytes 49168 | tf_op jit(solution)/shard_map/reduce_scatter | solution.py:119
  459.1 27.5 %all-reduce.9 = (bf16[16,18]{0,1:T(8,128)(2,1)S(1)}, bf16[16,3,512]{2,0,1:T(8,128)(2,1)S(1)}) all-reduce(bf16[16,18]{0,1:T(8,128)(2,1)S(1)} %copy.48, bf16[16,3,512]{2,0,1:T(8,128)(2,1)} %reduce-scatter.8.cloned.1.call-done), channel_id=1, replica_groups=mesh['tm'=32,'clip'=8] {'clip'}, use_global_device_ids=true, to_apply=%region_4.5 | all-reduce | flops 24864 | bytes 99456 | tf_op jit(solution)/shard_map/psum | solution.py:113
  488.0 190.9 %reduce-scatter.10.cloned.1.call-done = bf16[8,4608]{1,0:T(8,128)(2,1)} async-done(((bf16[256,4608]{1,0:T(8,128)(2,1)}), bf16[8,4608]{1,0:T(8,128)(2,1)}) %reduce-scatter.10.cloned.1.call-update) | async-done | bytes 73744
  678.9 1.6 convert_element_type.126
  (71 shorter events, 21.0 us)
Async XLA Ops:
  8.0 4.2 copy-start
  8.0 6.2 copy-start.7
  8.0 137.6 %all-gather.2.cloned.1.call-start = ((), (), s32[]{:S(2)}) async-start(), calls=%async_computation.4 | async-start | bytes 21233664 | tf_op jit(solution)/shard_map/all_gather | solution.py:108
  12.2 3.9 copy-start.5
  14.7 13.4 %collective-permute-start = (bf16[2,256,512]{2,1,0:T(8,128)(2,1)S(1)}, bf16[2,256,512]{2,1,0:T(8,128)(2,1)S(1)}, u32[]{:S(2)}, u32[]{:S(2)}) collective-permute-start(bf16[2,256,512]{2,1,0:T(8,128)(2,1)S(1)} %bitcast.259), channel_id=1, source_target_pairs={{8,0},{16,8},{24,16},{32,24},{40,32},{48,40},{56,48},{64,56},{72,6... | collective-permute-start | bytes 1572872 | tf_op jit(solution)/shard_map/ppermute | solution.py:13
  28.3 1.2 copy-start.1
  31.9 2.3 copy-start.6
  40.9 200.0 %reduce-scatter.12.cloned.1.call-start = ((), (), s32[]{:S(2)}) async-start(), calls=%async_computation.7 | async-start | bytes 135168
  42.0 417.1 %reduce-scatter.8.cloned.1.call-start = ((), (), s32[]{:S(2)}) async-start(), calls=%async_computation.5 | async-start | bytes 1622016 | tf_op jit(solution)/shard_map/reduce_scatter | solution.py:119
  42.1 1.9 copy-start.3
  43.7 6.2 copy-start.2
  44.0 6.5 copy-start.8
  44.2 15.1 %collective-permute-start.1 = (bf16[2,256,512]{2,1,0:T(8,128)(2,1)S(1)}, bf16[2,256,512]{2,1,0:T(8,128)(2,1)S(1)}, u32[]{:S(2)}, u32[]{:S(2)}) collective-permute-start(bf16[2,256,512]{2,1,0:T(8,128)(2,1)S(1)} %bitcast.257), channel_id=1, source_target_pairs={{0,8},{8,16},{16,24},{24,32},{32,40},{40,48},{48,56},{56,64},{64,7... | collective-permute-start | bytes 1572872 | tf_op jit(solution)/shard_map/ppermute | solution.py:13
  62.6 616.2 %reduce-scatter.10.cloned.1.call-start = ((), (), s32[]{:S(2)}) async-start(), calls=%async_computation.6 | async-start | bytes 2433024
  170.3 1.8 copy-start.4
  177.4 64.3 %all-to-all-start = ((bf16[1,4,256,256]{3,1,0,2:T(4,128)(2,1)}), bf16[1,4,256,256]{3,1,0,2:T(4,128)(2,1)S(1)}, u32[]{:S(2)}, u32[]{:S(2)}) async-start(bf16[1,4,256,256]{3,1,0,2:T(4,128)(2,1)} %copy.22), calls=%async_computation | async-start | bytes 1048576 | tf_op jit(solution)/shard_map/all_to_all | solution.py:103
Sparse Core Ops, SparseCore 0:
  41.0 104.5 all-gather.1
Sparse Core Ops, SparseCore 1:
  45.6 195.3 reduce-scatter.11
  245.1 214.0 reduce-scatter.7
  463.3 215.5 reduce-scatter.9
